TPU v7x, 256 devices: a whole 4x4x8 slice. The times are simulated.
256 devices in a mesh: dp: 4 (over y_lo, core), seq: 8 (over y_hi, x), head: 8 (over z).
Axes of the slice: x: 4, y: 4 (y_hi: 2, y_lo: 2; y = y_hi * 2 + y_lo), z: 8, core: 2. Of those that a mesh axis runs over, the one named last changes fastest.
Arguments:
- queries: bfloat16 [4, 2048, 3072], P('dp', 'seq', 'head'), may hold values from -160 to 160
- key_cache: bfloat16 [4, 2048, 1024], P('dp', 'seq', 'head'), may hold values from -7 to 7
- value_cache: bfloat16 [4, 2048, 1024], P('dp', 'seq', 'head'), may hold values from -6 to 6
- out_grad: bfloat16 [4, 2048, 3072], P('dp', 'seq', 'head'), may hold values from -6 to 6
- doc_ids: int32 [4, 2048], P('dp', 'seq'), may hold values from 0 to 1, never falling along the last dimension, each value on 1 to 2047 neighbouring positions
- layer_input: bfloat16 [4, 2048, 3072], P('dp', ('seq', 'head')), may hold values from -6 to 6
- key_proj: bfloat16 [3072, 1024], P(None, 'head'), may hold values from -0.109375 to 0.109375
- value_proj: bfloat16 [3072, 1024], P(None, 'head'), may hold values from -0.109375 to 0.109375
Outputs:
- query_grad: bfloat16 [4, 2048, 3072], P('dp', 'seq', 'head')
- input_grad: bfloat16 [4, 2048, 3072], P('dp', ('seq', 'head'))
- grad_keyproj: float32 [3072, 1024], P(None, 'head')
- grad_valueproj: float32 [3072, 1024], P(None, 'head')
Inputs may be any that keep to these rules, and one draw needn't show every extreme that they name: `doc_ids`: document numbers never fall along a sequence; a document spans 1 to 2047 positions.
All inputs are finite; a program needn't handle non-finite values.
Results may differ from a plain program's by a relative error of at most 0.02.
Values may be sent and summed in bfloat16 or wider, within the bound.
A program may use at most 64 MiB of HBM per device.

v0:
```python
import jax
import jax.numpy as jnp
from jax import lax
from jax.sharding import PartitionSpec as P

D = 3072
HD = 128
GROUP = 3
NEG_FILL = -1e30


def in_order(tiles, dim):
    shape = list(tiles.shape[1:])
    shape[dim] *= tiles.shape[0]
    return jnp.moveaxis(tiles, 0, dim).reshape(shape)


def sent_to_all(x, axis):
    peers = lax.axis_size(axis)
    return lax.all_to_all(jnp.broadcast_to(x[None], (peers, *x.shape)), axis, 0, 0, tiled=True)


def collect(x, axis, dim):
    return in_order(sent_to_all(x, axis), dim)


def in_blocks(x, dim, peers):
    shape = x.shape
    tiles = x.reshape(*shape[:dim], peers, shape[dim] // peers, *shape[dim + 1 :])
    return jnp.moveaxis(tiles, dim, 0)


def sum_at_owner(x, axis, dim):
    tiles = in_blocks(x, dim, lax.axis_size(axis))
    arrived = lax.all_to_all(tiles, axis, split_axis=0, concat_axis=0, tiled=True)
    return arrived.astype(jnp.float32).sum(axis=0)


def shards(queries, key_cache, value_cache, out_grad, doc_ids, layer_input, key_proj, value_proj):
    rows_query = queries.shape[1]
    col_width = key_cache.shape[2]
    kv_heads = col_width // HD
    cycle_size = lax.axis_size("seq")
    head_count = lax.axis_size("head")
    own_index = lax.axis_index("seq")
    score_scale = HD ** (-0.5)
    query_four = queries[0].reshape(rows_query, kv_heads, GROUP, HD)
    grad_four = out_grad[0].reshape(rows_query, kv_heads, GROUP, HD)
    own_blocks = jnp.stack([key_cache[0], value_cache[0]])
    all_docs = collect(doc_ids, "seq", 1)[0]
    query_doc = doc_ids[0]
    query_pos = own_index * rows_query + lax.iota(jnp.int32, rows_query)
    last_pos = own_index * rows_query + rows_query - 1

    def block_scores(kv_piece, row_start):
        row_total = kv_piece.shape[1]
        key_block = kv_piece[0].reshape(row_total, kv_heads, HD)
        value_block = kv_piece[1].reshape(row_total, kv_heads, HD)
        key_pos = row_start + lax.iota(jnp.int32, row_total)
        key_doc = lax.dynamic_slice_in_dim(all_docs, row_start, row_total)
        allowed = (key_pos[None, :] <= query_pos[:, None]) & (
            key_doc[None, :] == query_doc[:, None]
        )
        scores = (
            jnp.einsum("ihge,jhe->hgij", query_four, key_block, preferred_element_type=jnp.float32)
            * score_scale
        )
        masked = jnp.where(allowed, scores, NEG_FILL)
        weight_grad = jnp.einsum(
            "ihge,jhe->hgij", grad_four, value_block, preferred_element_type=jnp.float32
        )
        return (key_block, allowed, masked, weight_grad)

    def stats_block(state_in, kv_piece, row_start):
        row_top, row_sum, row_acc = state_in
        key_block, allowed, masked, weight_grad = block_scores(kv_piece, row_start)
        new_top = jnp.maximum(row_top, jnp.max(masked, axis=-1))
        weights = jnp.where(allowed, jnp.exp(masked - new_top[..., None]), 0.0)
        decay = jnp.exp(row_top - new_top)
        return (
            new_top,
            row_sum * decay + jnp.sum(weights, axis=-1),
            row_acc * decay + jnp.sum(weights * weight_grad, axis=-1),
        )

    def stats_fold(state_in, kv_piece, row_start):
        row_total = kv_piece.shape[1]
        sub_rows = min(row_total, rows_query)

        def one_part(part_num, state_mid):
            part_start = row_start + part_num * sub_rows
            sub_piece = kv_piece
            return lax.cond(
                part_start <= last_pos,
                lambda: stats_block(state_mid, sub_piece, part_start),
                lambda: state_mid,
            )

        return lax.fori_loop(0, row_total // sub_rows, one_part, state_in)

    stat_shape = (kv_heads, GROUP, rows_query)
    stats_init = (
        jnp.full(stat_shape, NEG_FILL, jnp.float32),
        jnp.zeros(stat_shape, jnp.float32),
        jnp.zeros(stat_shape, jnp.float32),
    )
    all_blocks = collect(own_blocks, "seq", 1)
    row_top, row_sum, row_acc = lax.fori_loop(
        0,
        cycle_size,
        lambda block_num, state_mid: stats_fold(
            state_mid,
            lax.dynamic_slice_in_dim(all_blocks, block_num * rows_query, rows_query, 1),
            block_num * rows_query,
        ),
        stats_init,
    )
    log_total = row_top + jnp.log(row_sum)
    row_delta = row_acc / row_sum

    def grad_block(kv_piece, row_start):
        row_total = kv_piece.shape[1]
        key_block, allowed, masked, weight_grad = block_scores(kv_piece, row_start)
        weights = jnp.where(allowed, jnp.exp(masked - log_total[..., None]), 0.0)
        score_grad = (weights * (weight_grad - row_delta[..., None]) * score_scale).astype(
            jnp.bfloat16
        )
        weights_low = weights.astype(jnp.bfloat16)
        query_add = jnp.einsum(
            "hgij,jhe->ihge", score_grad, key_block, preferred_element_type=jnp.float32
        )
        key_add = jnp.einsum(
            "hgij,ihge->jhe", score_grad, query_four, preferred_element_type=jnp.float32
        )
        value_add = jnp.einsum(
            "hgij,ihge->jhe", weights_low, grad_four, preferred_element_type=jnp.float32
        )
        return (
            query_add,
            jnp.stack(
                [key_add.reshape(row_total, col_width), value_add.reshape(row_total, col_width)]
            ),
        )

    zero_query = jnp.zeros((rows_query, kv_heads, GROUP, HD), jnp.float32)

    def guarded(kv_piece, row_start):
        return lax.cond(
            row_start <= last_pos,
            lambda: grad_block(kv_piece, row_start),
            lambda: (zero_query, jnp.zeros(kv_piece.shape, jnp.float32)),
        )

    def gathered_turn(block_num, state_mid):
        grad_terms, query_sum = state_mid
        row_start = block_num * rows_query
        kv_piece = lax.dynamic_slice_in_dim(all_blocks, row_start, rows_query, 1)
        query_add, kv_add = guarded(kv_piece, row_start)
        return (
            lax.dynamic_update_slice_in_dim(grad_terms, kv_add, row_start, 1),
            query_sum + query_add,
        )

    terms_init = jnp.zeros(all_blocks.shape, jnp.float32)
    grad_terms, query_sum = lax.fori_loop(0, cycle_size, gathered_turn, (terms_init, zero_query))
    kv_grads = sum_at_owner(grad_terms.astype(jnp.bfloat16), "seq", 1)
    query_grad = query_sum.astype(jnp.bfloat16).reshape(1, rows_query, kv_heads * GROUP * HD)
    kv_low = kv_grads.astype(jnp.bfloat16)
    input_rows = rows_query // head_count
    contract_cols = (((1,), (1,)), ((), ()))
    sub_grads = kv_low
    key_term = lax.dot_general(
        sub_grads[0], key_proj, contract_cols, preferred_element_type=jnp.float32
    )
    value_term = lax.dot_general(
        sub_grads[1], value_proj, contract_cols, preferred_element_type=jnp.float32
    )
    input_sum = lax.psum_scatter(
        (key_term + value_term).astype(jnp.bfloat16), "head", scatter_dimension=0, tiled=True
    )
    input_grad = input_sum.reshape(1, input_rows, D)
    contract_rows = (((0,), (0,)), ((), ()))
    input_piece = collect(layer_input[0], "head", 0)
    row_total = input_piece.shape[0]
    sub_grads = kv_low
    key_part = lax.dot_general(
        input_piece, sub_grads[0], contract_rows, preferred_element_type=jnp.float32
    )
    value_part = lax.dot_general(
        input_piece, sub_grads[1], contract_rows, preferred_element_type=jnp.float32
    )
    grad_keyproj, grad_valueproj = (
        lax.psum(key_part.astype(jnp.bfloat16), ("dp", "seq")).astype(jnp.float32),
        lax.psum(value_part.astype(jnp.bfloat16), ("dp", "seq")).astype(jnp.float32),
    )
    return (query_grad, input_grad, grad_keyproj, grad_valueproj)


def solution(mesh):
    return jax.shard_map(
        shards,
        mesh=mesh,
        in_specs=(
            P("dp", "seq", "head"),
            P("dp", "seq", "head"),
            P("dp", "seq", "head"),
            P("dp", "seq", "head"),
            P("dp", "seq"),
            P("dp", ("seq", "head"), None),
            P(None, "head"),
            P(None, "head"),
        ),
        out_specs=(
            P("dp", "seq", "head"),
            P("dp", ("seq", "head"), None),
            P(None, "head"),
            P(None, "head"),
        ),
        check_vma=False,
    )
```

profile of v0, /device:TPU:6, one launch (start us, length us, event | category | flops | bytes accessed | tf_op | source)
XLA Modules:
  0.0 297.8 jit_solution(2051672772160471777)
XLA Ops:
  8.0 1.0 pad_maximum_fusion.1
  9.2 22.5 %all_to_all.20 = bf16[8,2,256,128]{3,2,1,0:T(8,128)(2,1)S(1)} all-to-all(bf16[8,2,256,128]{3,2,1,0:T(8,128)(2,1)S(1)} %broadcast_in_dim.75), channel_id=1, replica_groups=mesh['dp'=4,'seq'=8,'head'=8] {'seq'}, dimensions={0} | all-to-all | bytes 2097152 | tf_op jit(solution)/shard_map/all_to_all | solution.py:20
  32.3 5.3 %all-to-all-start.1 = ((s32[8,1,256]{2,1,0:T(1,128)}), s32[8,1,256]{2,1,0:T(1,128)S(1)}, u32[]{:S(2)}, u32[]{:S(2)}) async-start(s32[8,1,256]{2,1,0:T(1,128)} %broadcast_in_dim.77), calls=%async_computation.1 | async-start | bytes 16384 | tf_op jit(solution)/shard_map/all_to_all | solution.py:20
  38.3 1.0 copy.41
  39.3 4.0 %all-to-all-done.1 = s32[8,1,256]{2,1,0:T(1,128)S(1)} async-done(((s32[8,1,256]{2,1,0:T(1,128)}), s32[8,1,256]{2,1,0:T(1,128)S(1)}, u32[]{:S(2)}, u32[]{:S(2)}) %all-to-all-start.1) | async-done | bytes 8224 | tf_op jit(solution)/shard_map/all_to_all | solution.py:20
  43.3 11.4 %while.49 = (s32[]{:T(128)}, f32[1,3,256]{2,1,0:T(4,128)S(1)}, f32[1,3,256]{2,1,0:T(4,128)S(1)}, f32[1,3,256]{2,1,0:T(4,128)S(1)}, s32[]{:T(128)}, /*index=5*/s3...) while((s32[]{:T(128)}, f32[1,3,256]{2,1,0:T(4,128)S(1)}, ...), condition=%wide.region_6.7_spmd.clone, body=%wide.region_0.6_spmd.clone.sunk | while | flops 102828800 | bytes 3211637 | solution.py:108
  43.3 2.8 conditional.6
  43.5 1.1 fusion.36
  44.7 1.2 fusion.7
  46.1 2.8 conditional.6
  46.3 1.1 fusion.36
  47.5 1.2 fusion.7
  48.9 2.8 conditional.6
  49.2 1.1 fusion.36
  50.3 1.2 fusion.7
  51.7 2.8 conditional.6
  52.0 1.1 fusion.36
  53.1 1.2 fusion.7
  54.7 1.0 broadcast_in_dim.73
  55.8 23.7 %while.50 = (s32[]{:T(128)}, bf16[2,2048,128]{2,1,0:T(8,128)(2,1)}, f32[256,1,3,128]{0,3,2,1:T(8,128)S(1)}, s32[]{:T(128)}, bf16[2,2048,128]{2,1,0:T(8,128)(2,1)...) while((s32[]{:T(128)}, bf16[2,2048,128]{2,1,0:T(8,128)(2,1)}, ...), condition=%wide.region_10.0_spmd.clone, body=%wide.region_7.10_spmd.clone.sunk | while | flops 253886976 | bytes 6900105 | solution.py:165
  55.8 4.2 %conditional.7 = (f32[256,1,3,128]{0,3,2,1:T(8,128)S(1)}, bf16[2,256,128]{2,1,0:T(8,128)(2,1)S(1)}) conditional(s32[]{:T(128)} %convert_element_type.80, () %tuple.114, (bf16[2,2048,128]{2,1,0:T(8,128)(2,1)}, s32[]{:T(128)}, s32[]{:T(128)}, s32[]{:T(128)}, s32[2048]{0:T(1024)S(1)}, /*index=5*/s32[1,256]{1,0:T(1,128)S(1)}, ...), branch_computations={%region_8.8_spmd, %region_9.9_spmd} | conditional | flops 253690368 | bytes 5456462 | solution.py:148
  56.0 1.2 fusion.21
  57.2 1.1 fusion.22
  58.3 1.1 convolution_bitcast_fusion.2
  60.8 4.2 %conditional.7 = (f32[256,1,3,128]{0,3,2,1:T(8,128)S(1)}, bf16[2,256,128]{2,1,0:T(8,128)(2,1)S(1)}) conditional(s32[]{:T(128)} %convert_element_type.80, () %tuple.114, (bf16[2,2048,128]{2,1,0:T(8,128)(2,1)}, s32[]{:T(128)}, s32[]{:T(128)}, s32[]{:T(128)}, s32[2048]{0:T(1024)S(1)}, /*index=5*/s32[1,256]{1,0:T(1,128)S(1)}, ...), branch_computations={%region_8.8_spmd, %region_9.9_spmd} | conditional | flops 253690368 | bytes 5456462 | solution.py:148
  61.0 1.2 fusion.21
  62.2 1.1 fusion.22
  63.3 1.1 convolution_bitcast_fusion.2
  65.8 4.2 %conditional.7 = (f32[256,1,3,128]{0,3,2,1:T(8,128)S(1)}, bf16[2,256,128]{2,1,0:T(8,128)(2,1)S(1)}) conditional(s32[]{:T(128)} %convert_element_type.80, () %tuple.114, (bf16[2,2048,128]{2,1,0:T(8,128)(2,1)}, s32[]{:T(128)}, s32[]{:T(128)}, s32[]{:T(128)}, s32[2048]{0:T(1024)S(1)}, /*index=5*/s32[1,256]{1,0:T(1,128)S(1)}, ...), branch_computations={%region_8.8_spmd, %region_9.9_spmd} | conditional | flops 253690368 | bytes 5456462 | solution.py:148
  66.0 1.2 fusion.21
  67.3 1.1 fusion.22
  68.4 1.1 convolution_bitcast_fusion.2
  70.8 4.2 %conditional.7 = (f32[256,1,3,128]{0,3,2,1:T(8,128)S(1)}, bf16[2,256,128]{2,1,0:T(8,128)(2,1)S(1)}) conditional(s32[]{:T(128)} %convert_element_type.80, () %tuple.114, (bf16[2,2048,128]{2,1,0:T(8,128)(2,1)}, s32[]{:T(128)}, s32[]{:T(128)}, s32[]{:T(128)}, s32[2048]{0:T(1024)S(1)}, /*index=5*/s32[1,256]{1,0:T(1,128)S(1)}, ...), branch_computations={%region_8.8_spmd, %region_9.9_spmd} | conditional | flops 253690368 | bytes 5456462 | solution.py:148
  71.1 1.2 fusion.21
  72.3 1.1 fusion.22
  73.4 1.1 convolution_bitcast_fusion.2
  79.4 1.3 copy.48
  80.8 44.8 %all_to_all.21 = bf16[8,2,256,128]{3,2,1,0:T(8,128)(2,1)} all-to-all(bf16[8,2,256,128]{3,2,1,0:T(8,128)(2,1)S(1)} %copy.48), channel_id=1, replica_groups=mesh['dp'=4,'seq'=8,'head'=8] {'seq'}, dimensions={0} | all-to-all | bytes 2097152 | tf_op jit(solution)/shard_map/all_to_all | solution.py:35
  125.5 1.3 broadcast_in_dim.80
  126.8 8.5 %all-to-all-start.3 = ((bf16[8,32,3072]{2,1,0:T(8,128)(2,1)}), bf16[8,32,3072]{2,1,0:T(8,128)(2,1)S(1)}, u32[]{:S(2)}, u32[]{:S(2)}) async-start(bf16[8,32,3072]{2,1,0:T(8,128)(2,1)} %broadcast_in_dim.80), calls=%async_computation.4 | async-start | bytes 3145728 | tf_op jit(solution)/shard_map/all_to_all | solution.py:20
  135.3 1.4 reduce_sum.34
  136.7 34.5 %all-to-all-done.3 = bf16[8,32,3072]{2,1,0:T(8,128)(2,1)S(1)} async-done(((bf16[8,32,3072]{2,1,0:T(8,128)(2,1)}), bf16[8,32,3072]{2,1,0:T(8,128)(2,1)S(1)}, u32[]{:S(2)}, u32[]{:S(2)}) %all-to-all-start.3) | async-done | bytes 1572896 | tf_op jit(solution)/shard_map/all_to_all | solution.py:20
  171.2 1.3 fusion.33
  172.5 1.3 fusion.34
  174.9 1.7 fusion.32
  177.5 108.8 %all-reduce.3.cloned.1.call-done = (bf16[3072,128]{0,1:T(8,128)(2,1)}, bf16[3072,128]{0,1:T(8,128)(2,1)}) async-done(((bf16[3072,128]{0,1:T(8,128)(2,1)}, bf16[3072,128]{0,1:T(8,128)(2,1)}), (bf16[3072,128]{0,1:T(8,128)(2,1)}, bf16[3072,128]{0,1:T(8,128)(2,1)})) %all-reduce.3.cloned.1.call-update) | async-done | bytes 1572880 | tf_op jit(solution)/shard_map/psum | solution.py:193
  286.4 2.6 copy.50
  289.0 1.4 copy.51
  (133 shorter events, 14.9 us)
Async XLA Ops:
  8.0 165.8 %copy-start = (bf16[3072,128]{1,0:T(8,128)(2,1)S(1)}, bf16[3072,128]{1,0:T(8,128)(2,1)}, u32[]{:S(2)}) copy-start(bf16[3072,128]{1,0:T(8,128)(2,1)} %param.22) | copy-start | bytes 2359300
  9.0 22.7 %copy-start.6 = (s32[1,256]{1,0:T(1,128)S(1)}, s32[1,256]{1,0:T(1,128)}, u32[]{:S(2)}) copy-start(s32[1,256]{1,0:T(1,128)} %param.20) | copy-start | bytes 3076
  9.0 28.6 %copy-start.4 = (bf16[1,256,384]{2,1,0:T(8,128)(2,1)S(1)}, bf16[1,256,384]{2,1,0:T(8,128)(2,1)}, u32[]{:S(2)}) copy-start(bf16[1,256,384]{2,1,0:T(8,128)(2,1)} %param.16) | copy-start | bytes 589828
  9.2 28.7 %copy-start.5 = (bf16[1,256,384]{2,1,0:T(8,128)(2,1)S(1)}, bf16[1,256,384]{2,1,0:T(8,128)(2,1)}, u32[]{:S(2)}) copy-start(bf16[1,256,384]{2,1,0:T(8,128)(2,1)} %param.19) | copy-start | bytes 589828
  32.3 10.9 %all-to-all-start.1 = ((s32[8,1,256]{2,1,0:T(1,128)}), s32[8,1,256]{2,1,0:T(1,128)S(1)}, u32[]{:S(2)}, u32[]{:S(2)}) async-start(s32[8,1,256]{2,1,0:T(1,128)} %broadcast_in_dim.77), calls=%async_computation.1 | async-start | bytes 16384 | tf_op jit(solution)/shard_map/all_to_all | solution.py:20
  80.7 44.8 %copy-start.3 = (bf16[1,32,3072]{2,1,0:T(8,128)(2,1)S(1)}, bf16[1,32,3072]{2,1,0:T(8,128)(2,1)}, u32[]{:S(2)}) copy-start(bf16[1,32,3072]{2,1,0:T(8,128)(2,1)} %param.21) | copy-start | bytes 589828
  126.8 44.3 %all-to-all-start.3 = ((bf16[8,32,3072]{2,1,0:T(8,128)(2,1)}), bf16[8,32,3072]{2,1,0:T(8,128)(2,1)S(1)}, u32[]{:S(2)}, u32[]{:S(2)}) async-start(bf16[8,32,3072]{2,1,0:T(8,128)(2,1)} %broadcast_in_dim.80), calls=%async_computation.4 | async-start | bytes 3145728 | tf_op jit(solution)/shard_map/all_to_all | solution.py:20
  135.3 151.1 %all-reduce.3.cloned.1.call-start = ((), (), s32[]{:S(2)}) async-start(), calls=%async_computation.6 | async-start | bytes 3145728 | tf_op jit(solution)/shard_map/psum | solution.py:193
  173.8 1.1 copy-start.2
  173.8 116.6 %reduce-scatter.2.cloned.1.call-start = ((), (), s32[]{:S(2)}) async-start(), calls=%async_computation.5 | async-start | bytes 1769472 | tf_op jit(solution)/shard_map/reduce_scatter | solution.py:178
  286.4 2.6 copy-start.1
Sparse Core Ops, SparseCore 0:
  173.9 112.4 all-reduce.2
Sparse Core Ops, SparseCore 1:
  177.4 34.9 reduce-scatter.1
where the time goes:
time: 300 us; the launch traced here: 298 us
  waiting for transfers between devices  147 us (49%)
  blocking collectives  67.3 us (22%)
  matrix products  29.5 us (10%)
  local copies, waits for them, and re-layouts  17.7 us (6%)
  between operations  15.6 us (5%)
  starting transfers between devices  13.8 us (5%)
  other arithmetic  5.27 us (2%)
    psum x1, waiting for transfers between devices, shards(): lax.psum(key_part.astype(jnp.bfloat16), ('dp', 'seq')).astype(jnp.float32)  109 us
    all_to_all x1, blocking collectives, sum_at_owner(): lax.all_to_all(tiles, axis, split_axis=0, concat_axis=0, tiled=True)  44.8 us
    all_to_all x2, waiting for transfers between devices, sent_to_all(): lax.all_to_all(jnp.broadcast_to(x[None], (peers, *x.shape)), axis, 0, 0,...  38.4 us
    all_to_all x1, blocking collectives, sent_to_all(): lax.all_to_all(jnp.broadcast_to(x[None], (peers, *x.shape)), axis, 0, 0,...  22.5 us
    all_to_all x2, starting transfers between devices, sent_to_all(): lax.all_to_all(jnp.broadcast_to(x[None], (peers, *x.shape)), axis, 0, 0,...  13.8 us
    dot_general x8, matrix products, block_scores(): jnp.einsum('ihge,jhe->hgij', query_four, key_block, preferred_element_typ...  9.29 us
    dot_general x8, matrix products, block_scores(): jnp.einsum('ihge,jhe->hgij', grad_four, value_block, preferred_element_ty...  9.06 us
  transfers between devices with their start and end apart: 4, of which 3 were waited for; matrix products, arithmetic and copies ran while one was open for 3% of the time, Pallas kernels for 0%

commit v1 on v0

--- a/solution.py
+++ b/solution.py
@@ -190,7 +190,7 @@
         input_piece, sub_grads[1], contract_rows, preferred_element_type=jnp.float32
     )
     grad_keyproj, grad_valueproj = (
-        lax.psum(key_part.astype(jnp.bfloat16), ("dp", "seq")).astype(jnp.float32),
+        lax.psum(lax.psum(key_part.astype(jnp.bfloat16), "seq"), "dp").astype(jnp.float32),
         lax.psum(value_part.astype(jnp.bfloat16), ("dp", "seq")).astype(jnp.float32),
     )
     return (query_grad, input_grad, grad_keyproj, grad_valueproj)

time: 300 us -> 436 us (1.45)
  waiting for transfers between devices: 147 us -> 281 us
    psum x1 -> x3, waiting for transfers between devices: 109 us -> 243 us  [the longest x1 116 us: shards(): lax.psum(value_part.astype(jnp.bfloat16), ('dp', 'seq')).astype(jnp.float32)]
  transfers between devices with their start and end apart: 4 -> 6, of which waited for: 3 -> 5; matrix products, arithmetic and copies ran while one was open for 3% -> 3% of each run, Pallas kernels for 0% -> 0%
where the time goes in v1:
time: 436 us; the launch traced here: 433 us
  waiting for transfers between devices  281 us (64%)
  blocking collectives  67.3 us (15%)
  matrix products  29.5 us (7%)
  local copies, waits for them, and re-layouts  18.8 us (4%)
  between operations  15.3 us (4%)
  starting transfers between devices  13.9 us (3%)
  other arithmetic  5.27 us (1%)
    psum x1, waiting for transfers between devices, shards(): lax.psum(value_part.astype(jnp.bfloat16), ('dp', 'seq')).astype(jnp.float32)  116 us
    psum x1, waiting for transfers between devices, shards(): lax.psum(key_part.astype(jnp.bfloat16), 'seq')  82.9 us
    all_to_all x1, blocking collectives, sum_at_owner(): lax.all_to_all(tiles, axis, split_axis=0, concat_axis=0, tiled=True)  44.8 us
    psum x1, waiting for transfers between devices, shards(): lax.psum(lax.psum(key_part.astype(jnp.bfloat16), 'seq'), 'dp')  43.5 us
    all_to_all x2, waiting for transfers between devices, sent_to_all(): lax.all_to_all(jnp.broadcast_to(x[None], (peers, *x.shape)), axis, 0, 0,...  38.4 us
    all_to_all x1, blocking collectives, sent_to_all(): lax.all_to_all(jnp.broadcast_to(x[None], (peers, *x.shape)), axis, 0, 0,...  22.5 us
    all_to_all x2, starting transfers between devices, sent_to_all(): lax.all_to_all(jnp.broadcast_to(x[None], (peers, *x.shape)), axis, 0, 0,...  13.8 us
    dot_general x8, matrix products, block_scores(): jnp.einsum('ihge,jhe->hgij', query_four, key_block, preferred_element_typ...  9.29 us
  transfers between devices with their start and end apart: 6, of which 5 were waited for; matrix products, arithmetic and copies ran while one was open for 3% of the time, Pallas kernels for 0%

profile of v1, /device:TPU:6, one launch (start us, length us, event | category | flops | bytes accessed | tf_op | source)
XLA Modules:
  0.0 432.7 jit_solution(16706484074518964936)
XLA Ops:
  9.2 22.5 %all_to_all.20 = bf16[8,2,256,128]{3,2,1,0:T(8,128)(2,1)S(1)} all-to-all(bf16[8,2,256,128]{3,2,1,0:T(8,128)(2,1)S(1)} %broadcast_in_dim.75), channel_id=1, replica_groups=mesh['dp'=4,'seq'=8,'head'=8] {'seq'}, dimensions={0} | all-to-all | bytes 2097152 | tf_op jit(solution)/shard_map/all_to_all | solution.py:20
  32.3 5.3 %all-to-all-start.1 = ((s32[8,1,256]{2,1,0:T(1,128)}), s32[8,1,256]{2,1,0:T(1,128)S(1)}, u32[]{:S(2)}, u32[]{:S(2)}) async-start(s32[8,1,256]{2,1,0:T(1,128)} %broadcast_in_dim.77), calls=%async_computation.1 | async-start | bytes 16384 | tf_op jit(solution)/shard_map/all_to_all | solution.py:20
  38.3 1.0 copy.41
  39.3 4.0 all-to-all-done.1
  43.3 11.4 %while.49 = (s32[]{:T(128)}, f32[1,3,256]{2,1,0:T(4,128)S(1)}, f32[1,3,256]{2,1,0:T(4,128)S(1)}, f32[1,3,256]{2,1,0:T(4,128)S(1)}, s32[]{:T(128)}, /*index=5*/s3...) while((s32[]{:T(128)}, f32[1,3,256]{2,1,0:T(4,128)S(1)}, ...), condition=%wide.region_6.7_spmd.clone, body=%wide.region_0.6_spmd.clone.sunk | while | flops 102828800 | bytes 3211637 | solution.py:108
  43.3 2.8 conditional.6
  43.5 1.1 fusion.36
  44.7 1.2 fusion.7
  46.1 2.8 conditional.6
  46.3 1.1 fusion.36
  47.5 1.2 fusion.7
  48.9 2.8 conditional.6
  49.2 1.1 fusion.36
  50.3 1.2 fusion.7
  51.7 2.8 conditional.6
  52.0 1.1 fusion.36
  53.1 1.2 fusion.7
  55.8 23.7 %while.50 = (s32[]{:T(128)}, bf16[2,2048,128]{2,1,0:T(8,128)(2,1)}, f32[256,1,3,128]{0,3,2,1:T(8,128)S(1)}, s32[]{:T(128)}, bf16[2,2048,128]{2,1,0:T(8,128)(2,1)...) while((s32[]{:T(128)}, bf16[2,2048,128]{2,1,0:T(8,128)(2,1)}, ...), condition=%wide.region_10.0_spmd.clone, body=%wide.region_7.10_spmd.clone.sunk | while | flops 253886976 | bytes 6900105 | solution.py:165
  55.8 4.2 conditional.7
  56.0 1.2 fusion.21
  57.2 1.1 fusion.22
  58.3 1.1 convolution_bitcast_fusion.2
  60.8 4.2 conditional.7
  61.0 1.2 fusion.21
  62.2 1.1 fusion.22
  63.3 1.1 convolution_bitcast_fusion.2
  65.8 4.2 conditional.7
  66.0 1.2 fusion.21
  67.3 1.1 fusion.22
  68.4 1.1 convolution_bitcast_fusion.2
  70.8 4.2 conditional.7
  71.1 1.2 fusion.21
  72.3 1.1 fusion.22
  73.4 1.1 convolution_bitcast_fusion.2
  79.4 1.3 copy.48
  80.8 44.8 %all_to_all.21 = bf16[8,2,256,128]{3,2,1,0:T(8,128)(2,1)} all-to-all(bf16[8,2,256,128]{3,2,1,0:T(8,128)(2,1)S(1)} %copy.48), channel_id=1, replica_groups=mesh['dp'=4,'seq'=8,'head'=8] {'seq'}, dimensions={0} | all-to-all | bytes 2097152 | tf_op jit(solution)/shard_map/all_to_all | solution.py:35
  125.5 1.3 broadcast_in_dim.80
  126.8 8.5 %all-to-all-start.3 = ((bf16[8,32,3072]{2,1,0:T(8,128)(2,1)}), bf16[8,32,3072]{2,1,0:T(8,128)(2,1)S(1)}, u32[]{:S(2)}, u32[]{:S(2)}) async-start(bf16[8,32,3072]{2,1,0:T(8,128)(2,1)} %broadcast_in_dim.80), calls=%async_computation.4 | async-start | bytes 3145728 | tf_op jit(solution)/shard_map/all_to_all | solution.py:20
  135.3 1.4 reduce_sum.34
  136.7 34.4 %all-to-all-done.3 = bf16[8,32,3072]{2,1,0:T(8,128)(2,1)S(1)} async-done(((bf16[8,32,3072]{2,1,0:T(8,128)(2,1)}), bf16[8,32,3072]{2,1,0:T(8,128)(2,1)S(1)}, u32[]{:S(2)}, u32[]{:S(2)}) %all-to-all-start.3) | async-done | bytes 1572896 | tf_op jit(solution)/shard_map/all_to_all | solution.py:20
  171.2 1.3 fusion.33
  172.5 1.3 fusion.34
  173.9 82.9 %all-reduce.4.cloned.1.call-done = bf16[3072,128]{0,1:T(8,128)(2,1)} async-done(((bf16[3072,128]{0,1:T(8,128)(2,1)}), bf16[3072,128]{0,1:T(8,128)(2,1)}) %all-reduce.4.cloned.1.call-update) | async-done | bytes 786448 | tf_op jit(solution)/shard_map/psum | solution.py:193
  257.9 1.7 fusion.32
  260.5 116.5 %all-reduce.8.cloned.1.call-done = bf16[3072,128]{0,1:T(8,128)(2,1)} async-done(((bf16[3072,128]{0,1:T(8,128)(2,1)}), bf16[3072,128]{0,1:T(8,128)(2,1)}) %all-reduce.8.cloned.1.call-update) | async-done | bytes 786448 | tf_op jit(solution)/shard_map/psum | solution.py:194
  377.0 2.5 copy.51
  379.5 43.5 %all-reduce.6.cloned.1.call-done = bf16[3072,128]{0,1:T(8,128)(2,1)} async-done(((bf16[3072,128]{0,1:T(8,128)(2,1)}), bf16[3072,128]{0,1:T(8,128)(2,1)}) %all-reduce.6.cloned.1.call-update) | async-done | bytes 786448 | tf_op jit(solution)/shard_map/psum | solution.py:193
  423.0 2.5 copy.50
  (137 shorter events, 17.0 us)
Async XLA Ops:
  8.0 248.8 %copy-start = (bf16[3072,128]{1,0:T(8,128)(2,1)S(1)}, bf16[3072,128]{1,0:T(8,128)(2,1)}, u32[]{:S(2)}) copy-start(bf16[3072,128]{1,0:T(8,128)(2,1)} %param.22) | copy-start | bytes 2359300
  9.0 22.7 %copy-start.5 = (s32[1,256]{1,0:T(1,128)S(1)}, s32[1,256]{1,0:T(1,128)}, u32[]{:S(2)}) copy-start(s32[1,256]{1,0:T(1,128)} %param.20) | copy-start | bytes 3076
  9.0 28.6 %copy-start.3 = (bf16[1,256,384]{2,1,0:T(8,128)(2,1)S(1)}, bf16[1,256,384]{2,1,0:T(8,128)(2,1)}, u32[]{:S(2)}) copy-start(bf16[1,256,384]{2,1,0:T(8,128)(2,1)} %param.16) | copy-start | bytes 589828
  9.2 28.7 %copy-start.4 = (bf16[1,256,384]{2,1,0:T(8,128)(2,1)S(1)}, bf16[1,256,384]{2,1,0:T(8,128)(2,1)}, u32[]{:S(2)}) copy-start(bf16[1,256,384]{2,1,0:T(8,128)(2,1)} %param.19) | copy-start | bytes 589828
  32.3 10.9 %all-to-all-start.1 = ((s32[8,1,256]{2,1,0:T(1,128)}), s32[8,1,256]{2,1,0:T(1,128)S(1)}, u32[]{:S(2)}, u32[]{:S(2)}) async-start(s32[8,1,256]{2,1,0:T(1,128)} %broadcast_in_dim.77), calls=%async_computation.1 | async-start | bytes 16384 | tf_op jit(solution)/shard_map/all_to_all | solution.py:20
  80.7 44.8 %copy-start.2 = (bf16[1,32,3072]{2,1,0:T(8,128)(2,1)S(1)}, bf16[1,32,3072]{2,1,0:T(8,128)(2,1)}, u32[]{:S(2)}) copy-start(bf16[1,32,3072]{2,1,0:T(8,128)(2,1)} %param.21) | copy-start | bytes 589828
  126.8 44.3 %all-to-all-start.3 = ((bf16[8,32,3072]{2,1,0:T(8,128)(2,1)}), bf16[8,32,3072]{2,1,0:T(8,128)(2,1)S(1)}, u32[]{:S(2)}, u32[]{:S(2)}) async-start(bf16[8,32,3072]{2,1,0:T(8,128)(2,1)} %broadcast_in_dim.80), calls=%async_computation.4 | async-start | bytes 3145728 | tf_op jit(solution)/shard_map/all_to_all | solution.py:20
  135.3 121.4 %all-reduce.4.cloned.1.call-start = ((), (), s32[]{:S(2)}) async-start(), calls=%async_computation.6 | async-start | bytes 1572864 | tf_op jit(solution)/shard_map/psum | solution.py:193
  172.5 204.5 %all-reduce.8.cloned.1.call-start = ((), (), s32[]{:S(2)}) async-start(), calls=%async_computation.8 | async-start | bytes 1572864 | tf_op jit(solution)/shard_map/psum | solution.py:194
  173.8 249.2 %all-reduce.6.cloned.1.call-start = ((), (), s32[]{:S(2)}) async-start(), calls=%async_computation.7 | async-start | bytes 1572864 | tf_op jit(solution)/shard_map/psum | solution.py:193
  256.8 1.1 copy-start.1
  256.8 168.8 %reduce-scatter.2.cloned.1.call-start = ((), (), s32[]{:S(2)}) async-start(), calls=%async_computation.5 | async-start | bytes 1769472 | tf_op jit(solution)/shard_map/reduce_scatter | solution.py:178
Sparse Core Ops, SparseCore 0:
  172.6 84.0 all-reduce.3
  260.9 116.0 all-reduce.7
  379.9 43.1 all-reduce.5
Sparse Core Ops, SparseCore 1:
  260.4 40.3 reduce-scatter.1
